TPU v7x, 256 devices: a whole 4x4x8 slice. The times are simulated.
256 devices in a mesh: seq: 128 (over z, x, y_hi, core), head: 2 (over y_lo).
Axes of the slice: x: 4, y: 4 (y_hi: 2, y_lo: 2; y = y_hi * 2 + y_lo), z: 8, core: 2. Of those that a mesh axis runs over, the one named last changes fastest.
Arguments:
- image_query: bfloat16 [16, 16, 1024, 128], P(None, 'head', 'seq'), may hold values from -120 to 120
- image_key: bfloat16 [16, 16, 1024, 128], P(None, 'head', 'seq'), may hold values from -7 to 7
- image_value: bfloat16 [16, 16, 1024, 128], P(None, 'head', 'seq'), may hold values from -6 to 6
- text_query: bfloat16 [16, 16, 512, 128], P(None, 'head', 'seq'), may hold values from -6 to 6
- text_key: bfloat16 [16, 16, 512, 128], P(None, 'head', 'seq'), may hold values from -6 to 6
- text_value: bfloat16 [16, 16, 512, 128], P(None, 'head', 'seq'), may hold values from -6 to 6
- out_weight: bfloat16 [2048, 3072], P('head'), may hold values from -0.125 to 0.125
- image_count: int32 [16], replicated, may hold values from 256 to 1024, as said below
- text_length: int32 [16], replicated, may hold values from 64 to 512, as said below
Outputs:
- image_out: bfloat16 [16, 1024, 3072], P('head', 'seq')
- text_out: bfloat16 [16, 512, 3072], P('head', 'seq')
Inputs may be any that keep to these rules, and one draw needn't show every extreme that they name: `image_count`: in every draw some image has all 1024 tokens valid. `text_length`: in every draw some image has all 512 text tokens valid.
All inputs are finite; a program needn't handle non-finite values.
Results may differ from a plain program's by a relative error of at most 0.012.
Values may be sent and summed in bfloat16 or wider, within the bound.
A program may use at most 64 MiB of HBM per device.

v0:
```python
import jax
import jax.numpy as jnp
from jax import lax
from jax.sharding import PartitionSpec as P


def joint_attend(
    queries, image_keys, image_values, text_keys, text_values, image_valid, text_valid, factor
):
    image_scores = (
        jnp.einsum("qd,kd->qk", queries, image_keys, preferred_element_type=jnp.float32) * factor
    )
    image_scores = jnp.where(image_valid[None, :], image_scores, -jnp.inf)
    text_scores = (
        jnp.einsum("qd,kd->qk", queries, text_keys, preferred_element_type=jnp.float32) * factor
    )
    text_scores = jnp.where(text_valid[None, :], text_scores, -jnp.inf)
    highest = jnp.maximum(
        jnp.max(image_scores, axis=1, keepdims=True), jnp.max(text_scores, axis=1, keepdims=True)
    )
    image_powers = jnp.exp(image_scores - highest)
    text_powers = jnp.exp(text_scores - highest)
    denominator = jnp.sum(image_powers, axis=1, keepdims=True) + jnp.sum(
        text_powers, axis=1, keepdims=True
    )
    image_probs = (image_powers / denominator).astype(jnp.bfloat16)
    text_probs = (text_powers / denominator).astype(jnp.bfloat16)
    mixed = jnp.dot(image_probs, image_values, preferred_element_type=jnp.float32)
    mixed = mixed + jnp.dot(text_probs, text_values, preferred_element_type=jnp.float32)
    return mixed.astype(jnp.bfloat16)


def body(
    image_query,
    image_key,
    image_value,
    text_query,
    text_key,
    text_value,
    out_weight,
    image_count,
    text_length,
):
    images, heads_local, image_rows, head_dim = image_query.shape
    text_rows = text_query.shape[2]
    pair_count = images * heads_local
    model_width = out_weight.shape[1]

    def flatten(tensor):
        return tensor.reshape(pair_count, tensor.shape[2], head_dim)

    def joined(tensor):
        return tensor.reshape(tensor.shape[0] * tensor.shape[1], head_dim)

    arrived = (
        lax.all_to_all(flatten(image_query), "seq", split_axis=0, concat_axis=0, tiled=True),
        lax.all_to_all(flatten(image_key), "seq", split_axis=0, concat_axis=0, tiled=True),
        lax.all_to_all(flatten(image_value), "seq", split_axis=0, concat_axis=0, tiled=True),
        lax.all_to_all(flatten(text_query), "seq", split_axis=0, concat_axis=0, tiled=True),
        lax.all_to_all(flatten(text_key), "seq", split_axis=0, concat_axis=0, tiled=True),
        lax.all_to_all(flatten(text_value), "seq", split_axis=0, concat_axis=0, tiled=True),
    )
    query_image = joined(arrived[0])
    key_image = joined(arrived[1])
    value_image = joined(arrived[2])
    query_text = joined(arrived[3])
    key_text = joined(arrived[4])
    value_text = joined(arrived[5])
    image_index = lax.axis_index("seq") // heads_local
    chosen = jnp.arange(images) == image_index
    count_here = jnp.sum(jnp.where(chosen, image_count, 0))
    length_here = jnp.sum(jnp.where(chosen, text_length, 0))
    image_valid = jnp.arange(key_image.shape[0]) < count_here
    text_valid = jnp.arange(key_text.shape[0]) < length_here
    factor = head_dim ** (-0.5)
    block_rows = min(512, query_image.shape[0])
    blocks = query_image.reshape(-1, block_rows, head_dim)

    def attend_block(query_block):
        return joint_attend(
            query_block,
            key_image,
            value_image,
            key_text,
            value_text,
            image_valid,
            text_valid,
            factor,
        )

    image_attended = lax.map(attend_block, blocks).reshape(-1, head_dim)
    text_attended = attend_block(query_text)
    returned = (
        lax.all_to_all(
            image_attended.reshape(pair_count, image_rows, head_dim),
            "seq",
            split_axis=0,
            concat_axis=0,
            tiled=True,
        ),
        lax.all_to_all(
            text_attended.reshape(pair_count, text_rows, head_dim),
            "seq",
            split_axis=0,
            concat_axis=0,
            tiled=True,
        ),
    )
    image_heads = returned[0].reshape(images, heads_local, image_rows, head_dim)
    text_heads = returned[1].reshape(images, heads_local, text_rows, head_dim)
    regrouped = (
        lax.all_to_all(image_heads, "head", split_axis=0, concat_axis=1, tiled=True),
        lax.all_to_all(text_heads, "head", split_axis=0, concat_axis=1, tiled=True),
    )
    weight_piece = lax.all_gather(out_weight, "head", axis=0, tiled=True)
    head_count = weight_piece.shape[0] // head_dim
    weight_block = weight_piece.reshape(head_count, head_dim, model_width)
    image_part = regrouped[0]
    text_part = regrouped[1]
    image_sum = jnp.einsum(
        "ihtd,hdo->ito", image_part, weight_block, preferred_element_type=jnp.float32
    )
    text_sum = jnp.einsum(
        "ihtd,hdo->ito", text_part, weight_block, preferred_element_type=jnp.float32
    )
    return (image_sum.astype(jnp.bfloat16), text_sum.astype(jnp.bfloat16))


def solution(mesh):
    placed = (
        P(None, "head", "seq", None),
        P(None, "head", "seq", None),
        P(None, "head", "seq", None),
        P(None, "head", "seq", None),
        P(None, "head", "seq", None),
        P(None, "head", "seq", None),
        P("head", None),
        P(),
        P(),
    )
    return jax.shard_map(
        body,
        mesh=mesh,
        in_specs=placed,
        out_specs=(P("head", "seq", None), P("head", "seq", None)),
        check_vma=False,
    )
```

profile of v0, /device:TPU:1, one launch (start us, length us, event | category | flops | bytes accessed | tf_op | source)
XLA Modules:
  0.0 227.3 jit_solution(6841859512227176991)
XLA Ops:
  7.2 0.0 copy-start.2
  7.2 0.0 copy-start.3
  7.2 0.0 copy-start.4
  7.2 0.0 all-gather.2.cloned.1.call-start
  7.2 0.7 all-gather.2.cloned.1.call-update
  7.9 0.1 copy-done.2
  8.1 29.1 %all_to_all.76 = bf16[128,4,128]{2,1,0:T(4,128)(2,1)S(1)} all-to-all(bf16[128,4,128]{2,1,0:T(4,128)(2,1)S(1)} %bitcast.96), channel_id=1, replica_groups=mesh['seq'=128,'head'=2] {'seq'}, dimensions={0} | all-to-all | bytes 262144 | tf_op jit(solution)/shard_map/all_to_all | solution.py:60
  37.2 6.3 %all-to-all-start.7 = ((bf16[128,4,128]{2,1,0:T(4,128)(2,1)}), bf16[128,4,128]{2,1,0:T(4,128)(2,1)S(1)}, u32[]{:S(2)}, u32[]{:S(2)}) async-start(bf16[128,4,128]{2,1,0:T(4,128)(2,1)} %bitcast.19), calls=%async_computation.7 | async-start | bytes 262144 | tf_op jit(solution)/shard_map/all_to_all | solution.py:59
  43.6 0.0 copy-done.3
  43.6 0.7 fusion.30
  44.3 12.4 %all-to-all-done.7 = bf16[128,4,128]{2,1,0:T(4,128)(2,1)S(1)} async-done(((bf16[128,4,128]{2,1,0:T(4,128)(2,1)}), bf16[128,4,128]{2,1,0:T(4,128)(2,1)S(1)}, u32[]{:S(2)}, u32[]{:S(2)}) %all-to-all-start.7) | async-done | bytes 131104 | tf_op jit(solution)/shard_map/all_to_all | solution.py:59
  56.7 0.0 copy-start.1
  56.7 6.3 %all-to-all-start.1 = ((bf16[128,8,128]{2,1,0:T(8,128)(2,1)}), bf16[128,8,128]{2,1,0:T(8,128)(2,1)S(1)}, u32[]{:S(2)}, u32[]{:S(2)}) async-start(bf16[128,8,128]{2,1,0:T(8,128)(2,1)} %bitcast.2), calls=%async_computation.1 | async-start | bytes 524288 | tf_op jit(solution)/shard_map/all_to_all | solution.py:57
  63.0 0.6 iota_compare_fusion.3
  63.6 0.0 copy-done.4
  63.6 0.7 fusion.29
  64.3 0.7 iota_compare_fusion.2
  65.0 0.3 fusion.37
  65.3 12.8 %all-to-all-done.1 = bf16[128,8,128]{2,1,0:T(8,128)(2,1)S(1)} async-done(((bf16[128,8,128]{2,1,0:T(8,128)(2,1)}), bf16[128,8,128]{2,1,0:T(8,128)(2,1)S(1)}, u32[]{:S(2)}, u32[]{:S(2)}) %all-to-all-start.1) | async-done | bytes 262176 | tf_op jit(solution)/shard_map/all_to_all | solution.py:57
  78.1 0.0 copy-done.1
  78.1 8.2 %all-to-all-start.3 = ((bf16[128,8,128]{2,1,0:T(8,128)(2,1)}), bf16[128,8,128]{2,1,0:T(8,128)(2,1)}, u32[]{:S(2)}, u32[]{:S(2)}) async-start(bf16[128,8,128]{2,1,0:T(8,128)(2,1)} %bitcast.6), calls=%async_computation.3 | async-start | bytes 524288 | tf_op jit(solution)/shard_map/all_to_all | solution.py:58
  86.3 1.4 fusion.23
  87.7 0.2 fusion.28
  87.9 0.6 fusion.24
  88.5 12.6 %all-to-all-done.3 = bf16[128,8,128]{2,1,0:T(8,128)(2,1)} async-done(((bf16[128,8,128]{2,1,0:T(8,128)(2,1)}), bf16[128,8,128]{2,1,0:T(8,128)(2,1)}, u32[]{:S(2)}, u32[]{:S(2)}) %all-to-all-start.3) | async-done | bytes 262176 | tf_op jit(solution)/shard_map/all_to_all | solution.py:58
  101.1 8.2 %all-to-all-start.4 = ((bf16[128,4,128]{2,1,0:T(4,128)(2,1)}), bf16[128,4,128]{2,1,0:T(4,128)(2,1)}, u32[]{:S(2)}, u32[]{:S(2)}) async-start(bf16[128,4,128]{2,1,0:T(4,128)(2,1)} %bitcast.97), calls=%async_computation.4 | async-start | bytes 262144 | tf_op jit(solution)/shard_map/all_to_all | solution.py:61
  109.3 2.3 %fusion.27 = f32[512,128]{1,0:T(8,128)} fusion(f32[512,1024]{1,0:T(8,128)S(1)} %get-tuple-element.104, f32[512]{0:T(512)S(1)} %add.26, f32[512]{0:T(512)S(1)} %max.16, pred[1024]{0:T(1024)(128)(4,1)S(1)} %iota_compare_fusion.2, bf16[128,8,128]{2,1,0:T(8,128)(2,1)} %all-to-all-done.3), kind=kOutput, calls=%fused_computation.43 | convolution fusion | flops 136839168 | bytes 2626560 | tf_op jit(solution)/shard_map/dot_general | solution.py:28
  111.6 10.5 %all-to-all-done.4 = bf16[128,4,128]{2,1,0:T(4,128)(2,1)} async-done(((bf16[128,4,128]{2,1,0:T(4,128)(2,1)}), bf16[128,4,128]{2,1,0:T(4,128)(2,1)}, u32[]{:S(2)}, u32[]{:S(2)}) %all-to-all-start.4) | async-done | bytes 131104 | tf_op jit(solution)/shard_map/all_to_all | solution.py:61
  122.1 1.4 fusion.26
  123.5 18.7 %all_to_all.77 = bf16[128,4,128]{2,1,0:T(4,128)(2,1)S(1)} all-to-all(bf16[128,4,128]{2,1,0:T(4,128)(2,1)S(1)} %bitcast.98), channel_id=1, replica_groups=mesh['seq'=128,'head'=2] {'seq'}, dimensions={0} | all-to-all | bytes 262144 | tf_op jit(solution)/shard_map/all_to_all | solution.py:101
  142.1 6.3 %all-to-all-start = ((bf16[128,8,128]{2,1,0:T(8,128)(2,1)}), bf16[128,8,128]{2,1,0:T(8,128)(2,1)S(1)}, u32[]{:S(2)}, u32[]{:S(2)}) async-start(bf16[128,8,128]{2,1,0:T(8,128)(2,1)} %bitcast), calls=%async_computation | async-start | bytes 524288 | tf_op jit(solution)/shard_map/all_to_all | solution.py:56
  148.5 0.7 copy.22
  149.2 14.5 %all-to-all-done = bf16[128,8,128]{2,1,0:T(8,128)(2,1)S(1)} async-done(((bf16[128,8,128]{2,1,0:T(8,128)(2,1)}), bf16[128,8,128]{2,1,0:T(8,128)(2,1)S(1)}, u32[]{:S(2)}, u32[]{:S(2)}) %all-to-all-start) | async-done | bytes 262176 | tf_op jit(solution)/shard_map/all_to_all | solution.py:56
  163.7 3.4 %all-to-all-start.9 = ((bf16[16,8,4,128]{3,1,2,0:T(8,128)(2,1)}), bf16[16,8,4,128]{3,1,2,0:T(8,128)(2,1)S(1)}, u32[]{:S(2)}, u32[]{:S(2)}) async-start(bf16[16,8,4,128]{3,1,2,0:T(8,128)(2,1)} %copy.22), calls=%async_computation.9 | async-start | bytes 262144 | tf_op jit(solution)/shard_map/all_to_all | solution.py:113
  167.0 11.8 %while.11 = (s32[]{:T(128)}, bf16[2,512,128]{2,1,0:T(8,128)(2,1)S(1)}, bf16[2,512,128]{2,1,0:T(8,128)(2,1)S(1)}, bf16[1024,128]{1,0:T(8,128)(2,1)S(1)}, bf16[512...) while((s32[]{:T(128)}, ...), condition=%wide.region_7.8_spmd.clone, body=%wide.region_2.7_spmd.clone.sunk | while | flops 411173376 | bytes 11179137 | solution.py:91
  167.1 0.7 iota_compare_fusion.6
  167.7 0.5 fusion.64
  168.3 0.6 iota_compare_fusion.7
  168.9 0.3 fusion.65
  169.2 0.6 fusion.66
  169.8 0.2 fusion.67
  170.0 1.6 fusion.68
  171.6 1.3 fusion.69
  173.0 0.7 iota_compare_fusion.6
  173.6 0.5 fusion.64
  174.2 0.6 iota_compare_fusion.7
  174.8 0.3 fusion.65
  175.1 0.6 fusion.66
  175.7 0.2 fusion.67
  175.9 1.6 fusion.68
  177.5 1.3 fusion.69
  178.9 0.0 all-to-all-done.9
  178.9 22.3 %all_to_all.78 = bf16[128,8,128]{2,1,0:T(8,128)(2,1)} all-to-all(bf16[128,8,128]{2,1,0:T(8,128)(2,1)S(1)} %bitcast.95), channel_id=1, replica_groups=mesh['seq'=128,'head'=2] {'seq'}, dimensions={0} | all-to-all | bytes 524288 | tf_op jit(solution)/shard_map/all_to_all | solution.py:94
  201.2 3.7 %all-to-all-start.6 = ((bf16[16,8,8,128]{3,2,1,0:T(8,128)(2,1)}), bf16[16,8,8,128]{3,2,1,0:T(8,128)(2,1)S(1)}, u32[]{:S(2)}, u32[]{:S(2)}) async-start(bf16[16,8,8,128]{3,2,1,0:T(8,128)(2,1)} %bitcast.11), calls=%async_computation.6 | async-start | bytes 524288 | tf_op jit(solution)/shard_map/all_to_all | solution.py:112
  204.8 0.1 copy.23
  204.9 4.2 %all-to-all-done.6 = bf16[16,8,8,128]{3,2,1,0:T(8,128)(2,1)S(1)} async-done(((bf16[16,8,8,128]{3,2,1,0:T(8,128)(2,1)}), bf16[16,8,8,128]{3,2,1,0:T(8,128)(2,1)S(1)}, u32[]{:S(2)}, u32[]{:S(2)}) %all-to-all-start.6) | async-done | bytes 262176 | tf_op jit(solution)/shard_map/all_to_all | solution.py:112
  209.1 0.0 all-gather.2.cloned.1.call-done
  209.1 0.0 copy-start
  209.2 7.3 %fusion.21 = bf16[8,8,3072]{2,1,0:T(8,128)(2,1)} fusion(bf16[8,16,8,128]{3,2,1,0:T(8,128)(2,1)S(1)} %bitcast.88, bf16[16,128,3072,1]{2,1,0,3:T(8,128)(2,1)} %bitcast.82), kind=kOutput, calls=%fused_computation.29 | convolution fusion | flops 805502976 | bytes 13238272 | tf_op jit(solution)/shard_map/ihtd,hdo->ito/dot_general | solution.py:120
  216.5 1.0 copy-done
  217.5 2.2 fusion.22
  219.6 0.8 copy.24
  (8 shorter events, 0.1 us)
Async XLA Ops:
  7.2 0.9 copy-start.2
  7.2 36.4 %copy-start.3 = (s32[16]{0:T(128)S(1)}, s32[16]{0:T(128)}, u32[]{:S(2)}) copy-start(s32[16]{0:T(128)} %param.19) | copy-start | bytes 196
  7.2 56.4 %copy-start.4 = (s32[16]{0:T(128)S(1)}, s32[16]{0:T(128)}, u32[]{:S(2)}) copy-start(s32[16]{0:T(128)} %param.18) | copy-start | bytes 196
  7.2 201.9 %all-gather.2.cloned.1.call-start = ((), (), s32[]{:S(2)}) async-start(), calls=%async_computation.10 | async-start | bytes 18874368 | tf_op jit(solution)/shard_map/all_gather | solution.py:115
  37.2 19.5 %all-to-all-start.7 = ((bf16[128,4,128]{2,1,0:T(4,128)(2,1)}), bf16[128,4,128]{2,1,0:T(4,128)(2,1)S(1)}, u32[]{:S(2)}, u32[]{:S(2)}) async-start(bf16[128,4,128]{2,1,0:T(4,128)(2,1)} %bitcast.19), calls=%async_computation.7 | async-start | bytes 262144 | tf_op jit(solution)/shard_map/all_to_all | solution.py:59
  56.7 21.5 %copy-start.1 = (bf16[128,4,128]{2,1,0:T(4,128)(2,1)}, bf16[128,4,128]{2,1,0:T(4,128)(2,1)S(1)}, u32[]{:S(2)}) copy-start(bf16[128,4,128]{2,1,0:T(4,128)(2,1)S(1)} %all-to-all-done.7) | copy-start | bytes 393220
  56.7 21.5 %all-to-all-start.1 = ((bf16[128,8,128]{2,1,0:T(8,128)(2,1)}), bf16[128,8,128]{2,1,0:T(8,128)(2,1)S(1)}, u32[]{:S(2)}, u32[]{:S(2)}) async-start(bf16[128,8,128]{2,1,0:T(8,128)(2,1)} %bitcast.2), calls=%async_computation.1 | async-start | bytes 524288 | tf_op jit(solution)/shard_map/all_to_all | solution.py:57
  78.1 23.0 %all-to-all-start.3 = ((bf16[128,8,128]{2,1,0:T(8,128)(2,1)}), bf16[128,8,128]{2,1,0:T(8,128)(2,1)}, u32[]{:S(2)}, u32[]{:S(2)}) async-start(bf16[128,8,128]{2,1,0:T(8,128)(2,1)} %bitcast.6), calls=%async_computation.3 | async-start | bytes 524288 | tf_op jit(solution)/shard_map/all_to_all | solution.py:58
  101.1 21.0 %all-to-all-start.4 = ((bf16[128,4,128]{2,1,0:T(4,128)(2,1)}), bf16[128,4,128]{2,1,0:T(4,128)(2,1)}, u32[]{:S(2)}, u32[]{:S(2)}) async-start(bf16[128,4,128]{2,1,0:T(4,128)(2,1)} %bitcast.97), calls=%async_computation.4 | async-start | bytes 262144 | tf_op jit(solution)/shard_map/all_to_all | solution.py:61
  142.1 21.5 %all-to-all-start = ((bf16[128,8,128]{2,1,0:T(8,128)(2,1)}), bf16[128,8,128]{2,1,0:T(8,128)(2,1)S(1)}, u32[]{:S(2)}, u32[]{:S(2)}) async-start(bf16[128,8,128]{2,1,0:T(8,128)(2,1)} %bitcast), calls=%async_computation | async-start | bytes 524288 | tf_op jit(solution)/shard_map/all_to_all | solution.py:56
  163.7 15.2 %all-to-all-start.9 = ((bf16[16,8,4,128]{3,1,2,0:T(8,128)(2,1)}), bf16[16,8,4,128]{3,1,2,0:T(8,128)(2,1)S(1)}, u32[]{:S(2)}, u32[]{:S(2)}) async-start(bf16[16,8,4,128]{3,1,2,0:T(8,128)(2,1)} %copy.22), calls=%async_computation.9 | async-start | bytes 262144 | tf_op jit(solution)/shard_map/all_to_all | solution.py:113
  201.2 7.9 %all-to-all-start.6 = ((bf16[16,8,8,128]{3,2,1,0:T(8,128)(2,1)}), bf16[16,8,8,128]{3,2,1,0:T(8,128)(2,1)S(1)}, u32[]{:S(2)}, u32[]{:S(2)}) async-start(bf16[16,8,8,128]{3,2,1,0:T(8,128)(2,1)} %bitcast.11), calls=%async_computation.6 | async-start | bytes 524288 | tf_op jit(solution)/shard_map/all_to_all | solution.py:112
  209.1 8.3 %copy-start = (bf16[2048,3072]{1,0:T(8,128)(2,1)S(1)}, bf16[2048,3072]{1,0:T(8,128)(2,1)}, u32[]{:S(2)}) copy-start(bf16[2048,3072]{1,0:T(8,128)(2,1)} %all-gather.2.cloned.1.call-done) | copy-start | bytes 37748740
Sparse Core Ops, SparseCore 0:
  9.8 175.4 all-gather.1
where the time goes:
time: 229 us; the launch traced here: 227 us
  blocking collectives  70.1 us (31%)
  waiting for transfers between devices  67.7 us (30%)
  starting transfers between devices  42.4 us (19%)
  matrix products  22.5 us (10%)
  between operations  14.2 us (6%)
  other arithmetic  7.57 us (3%)
  local copies, waits for them, and re-layouts  2.73 us (1%)
    all_to_all x1, blocking collectives, body(): lax.all_to_all(flatten(text_key), 'seq', split_axis=0, concat_axis=0, til...  29.1 us
    all_to_all x1, blocking collectives, body(): lax.all_to_all(image_attended.reshape(pair_count, image_rows, head_dim),...  22.3 us
    all_to_all x1, blocking collectives, body(): lax.all_to_all(text_attended.reshape(pair_count, text_rows, head_dim), 's...  18.7 us
    all_to_all x1, waiting for transfers between devices, body(): lax.all_to_all(flatten(image_query), 'seq', split_axis=0, concat_axis=0,...  14.5 us
    all_to_all x1, waiting for transfers between devices, body(): lax.all_to_all(flatten(image_key), 'seq', split_axis=0, concat_axis=0, ti...  12.8 us
    all_to_all x1, waiting for transfers between devices, body(): lax.all_to_all(flatten(image_value), 'seq', split_axis=0, concat_axis=0,...  12.6 us
    all_to_all x1, waiting for transfers between devices, body(): lax.all_to_all(flatten(text_query), 'seq', split_axis=0, concat_axis=0, t...  12.4 us
    all_to_all x1, waiting for transfers between devices, body(): lax.all_to_all(flatten(text_value), 'seq', split_axis=0, concat_axis=0, t...  10.5 us
  transfers between devices with their start and end apart: 8, of which 6 were waited for; matrix products, arithmetic and copies ran while one was open for 9% of the time, Pallas kernels for 0%

commit v1 on v0

v1 whole, which is shorter than its diff:
```python
import functools

import jax
import jax.numpy as jnp
from jax import lax
from jax.experimental import pallas as pl
from jax.experimental.pallas import tpu as pltpu
from jax.sharding import PartitionSpec as P

MESH = pl.DeviceIdType.MESH
BF16 = jnp.bfloat16
F32 = jnp.float32

PLANES = 8
SLOTS = 16
HD = 128
IT, TT = 8, 4
CHUNK = SLOTS * (IT + TT)
IMG_KEYS = PLANES * SLOTS * IT
TXT_KEYS = PLANES * SLOTS * TT
KEYS = IMG_KEYS + TXT_KEYS
ROWS = 48
COLS = 512


def merge(block):
    wide = block.astype(F32)
    rows = 1
    for extent in block.shape[:-1]:
        rows *= extent
    return wide.reshape(rows, block.shape[-1]).astype(BF16)


def kernel(
    iq, ik, iv, tq, tk, tv, weight, counts, lengths,
    out_image, out_text,
    a_ik, a_tk, a_iq, a_tq, a_iv, a_tv,
    b_ik, b_tk, b_iq, b_tq, b_iv, b_tv,
    keys, values, powers, inverse,
    s_img, s_txt, c_img, c_txt, d_img, d_txt,
    w_vmem, lhs, part_send, part_recv, part_own,
    a_send, a_recv, b_send, b_recv, c_send, c_recv, d_send, d_recv,
    y_send, y_recv, w_sem, own_sem,
):
    seq = lax.axis_index("seq")
    eta = lax.axis_index("head")
    z, q = seq // SLOTS, seq % SLOTS
    width = weight.shape[1]
    steps = width // COLS

    def plane_peer(step):
        qx = (q // 4 + step // 4) % 4
        qy = ((q // 2) % 2 + (step // 2) % 2) % 2
        qc = (q % 2 + step % 2) % 2
        return qx * 4 + qy * 2 + qc

    def flipped(slot):
        return slot + 2 - 4 * ((slot // 2) % 2)

    def z_device(plane):
        return (plane * SLOTS + q, eta)

    def q_device(slot):
        return (z * SLOTS + slot, eta)

    partner_direct = (seq, 1 - eta)
    partner_flipped = (z * SLOTS + flipped(q), 1 - eta)

    barrier = pltpu.get_barrier_semaphore()

    def greet_z(step, carry):
        pl.semaphore_signal(
            barrier, inc=1, device_id=z_device((z + step) % PLANES), device_id_type=MESH
        )
        return carry

    def greet_q(step, carry):
        pl.semaphore_signal(
            barrier, inc=1, device_id=q_device(plane_peer(step)), device_id_type=MESH
        )
        return carry

    lax.fori_loop(1, PLANES, greet_z, 0)
    lax.fori_loop(1, SLOTS, greet_q, 0)
    pl.semaphore_signal(barrier, inc=1, device_id=partner_direct, device_id_type=MESH)
    pl.semaphore_signal(barrier, inc=1, device_id=partner_flipped, device_id_type=MESH)
    pl.semaphore_wait(barrier, PLANES - 1 + SLOTS - 1 + 2)

    def remote(src, dst, send, recv, device):
        return pltpu.make_async_remote_copy(
            src_ref=src, dst_ref=dst, send_sem=send, recv_sem=recv,
            device_id=device, device_id_type=MESH,
        )

    first = ((ik, a_ik), (tk, a_tk), (iq, a_iq), (tq, a_tq), (iv, a_iv), (tv, a_tv))
    second = (b_ik, b_tk, b_iq, b_tq, b_iv, b_tv)

    def start_a(n):
        src, dst = first[n]

        def body(step, carry):
            plane = (z + step) % PLANES
            remote(
                src.at[plane], dst.at[z], a_send.at[n], a_recv.at[n], z_device(plane)
            ).start()
            return carry

        lax.fori_loop(1, PLANES, body, 0)
        pltpu.make_async_copy(src.at[z], dst.at[z], own_sem.at[n]).start()

    def wait_a(n):
        src, dst = first[n]
        some = dst.at[pl.ds(0, PLANES - 1)]
        remote(some, some, a_send.at[n], a_recv.at[n], z_device(z)).wait_recv()
        pltpu.make_async_copy(src.at[z], dst.at[z], own_sem.at[n]).wait()

    def start_b(n):
        src, dst = first[n][1], second[n]

        def body(step, carry):
            slot = plane_peer(step)
            remote(
                src.at[:, slot], dst.at[:, q], b_send.at[n], b_recv.at[n], q_device(slot)
            ).start()
            return carry

        lax.fori_loop(1, SLOTS, body, 0)
        pltpu.make_async_copy(src.at[:, q], dst.at[:, q], own_sem.at[6 + n]).start()

    def wait_b(n):
        src, dst = first[n][1], second[n]
        some = dst.at[:, pl.ds(0, SLOTS - 1)]
        remote(some, some, b_send.at[n], b_recv.at[n], q_device(q)).wait_recv()
        pltpu.make_async_copy(src.at[:, q], dst.at[:, q], own_sem.at[6 + n]).wait()

    for n in range(6):
        start_a(n)
    load = pltpu.make_async_copy(weight, w_vmem, w_sem)
    load.start()
    for n in range(4):
        wait_a(n)
        start_b(n)

    image = 2 * z + q // 8
    count, length = counts[image], lengths[image]
    position = lax.broadcasted_iota(jnp.int32, (1, KEYS), 1)
    limit = jnp.where(position < IMG_KEYS, count, IMG_KEYS + length)
    bias = jnp.where(position < limit, 0.0, -1e30).astype(F32)

    wait_b(0)
    wait_b(1)
    keys[0:IMG_KEYS] = merge(b_ik[...])
    keys[IMG_KEYS:KEYS] = merge(b_tk[...])
    wait_b(2)
    wait_b(3)

    factor = HD**-0.5 * 1.4426950408889634

    def score(chunk, carry):
        rows = jnp.concatenate([merge(b_iq[chunk]), merge(b_tq[chunk])], axis=0)
        scores = lax.dot_general(
            rows, keys[...], (((1,), (1,)), ((), ())), preferred_element_type=F32
        )
        scores = scores + bias
        highest = jnp.max(scores, axis=1, keepdims=True)
        power = jnp.exp2((scores - highest) * factor)
        total = jnp.sum(power, axis=1, keepdims=True)
        powers[chunk] = power.astype(BF16)
        inverse[chunk] = jnp.broadcast_to(1.0 / total, (CHUNK, HD))
        return carry

    lax.fori_loop(0, PLANES, score, 0)

    for n in (4, 5):
        wait_a(n)
        start_b(n)
    wait_b(4)
    wait_b(5)
    values[0:IMG_KEYS] = merge(b_iv[...])
    values[IMG_KEYS:KEYS] = merge(b_tv[...])

    def attend(plane):
        mixed = jnp.dot(powers[plane], values[...], preferred_element_type=F32)
        mixed = mixed * inverse[plane]
        image_rows = mixed[0 : SLOTS * IT].reshape(SLOTS, IT, HD).astype(BF16)
        text_rows = mixed[SLOTS * IT : CHUNK].reshape(SLOTS, TT, HD).astype(BF16)
        return image_rows, text_rows

    def send_back(step, carry):
        plane = (z + step) % PLANES
        image_rows, text_rows = attend(plane)
        s_img[plane] = image_rows
        s_txt[plane] = text_rows
        remote(
            s_img.at[plane], c_img.at[z], c_send.at[0], c_recv.at[0], z_device(plane)
        ).start()
        remote(
            s_txt.at[plane], c_txt.at[z], c_send.at[1], c_recv.at[1], z_device(plane)
        ).start()
        return carry

    lax.fori_loop(1, PLANES, send_back, 0)
    image_rows, text_rows = attend(z)
    c_img[z] = image_rows
    c_txt[z] = text_rows

    near, far = 2 * eta, 6 - 6 * eta

    def ranges(src, dst, slot):
        return (
            (src.at[pl.ds(near, 6), slot], dst.at[q, pl.ds(near, 6)]),
            (src.at[pl.ds(far, 2), flipped(slot)], dst.at[q, pl.ds(far, 2)]),
        )

    for n, (src, dst) in enumerate(((c_txt, d_txt), (c_img, d_img))):
        m = 1 - n
        some = src.at[pl.ds(0, PLANES - 1)]
        remote(some, some, c_send.at[m], c_recv.at[m], z_device(z)).wait_recv()

        def share(step, carry, src=src, dst=dst, n=n):
            slot = plane_peer(step)
            for a, b in ranges(src, dst, slot):
                remote(a, b, d_send.at[n], d_recv.at[n], q_device(slot)).start()
            return carry

        lax.fori_loop(1, SLOTS, share, 0)
        for m, (a, b) in enumerate(ranges(src, dst, q)):
            pltpu.make_async_copy(a, b, own_sem.at[12 + 2 * n + m]).start()
    load.wait()
    for n, (src, dst) in enumerate(((c_txt, d_txt), (c_img, d_img))):
        some = dst.at[pl.ds(0, SLOTS - 1)]
        remote(some, some, d_send.at[n], d_recv.at[n], q_device(q)).wait_recv()
        for m, (a, b) in enumerate(ranges(src, dst, q)):
            pltpu.make_async_copy(a, b, own_sem.at[12 + 2 * n + m]).wait()

    bases = ((4 - 2 * eta, far), (2 + 2 * eta, 6 * eta))
    for side in range(2):
        for half in range(2):
            base = bases[side][half]
            for head in range(8):
                rows = jnp.concatenate(
                    [
                        d_img[parity * 8 + head, pl.ds(base, 2)].astype(F32).reshape(16, HD)
                        for parity in range(2)
                    ]
                    + [
                        d_txt[parity * 8 + head, pl.ds(base, 2)].astype(F32).reshape(8, HD)
                        for parity in range(2)
                    ],
                    axis=0,
                )
                lhs[
                    side, half * ROWS : (half + 1) * ROWS, head * HD : (head + 1) * HD
                ] = rows.astype(BF16)

    for step in range(steps):
        columns = pl.ds(step * COLS, COLS)
        part = jnp.dot(lhs[0], w_vmem[:, columns], preferred_element_type=F32)
        part_send[step] = part.astype(BF16).reshape(2, ROWS, COLS)
        for half, device in enumerate((partner_direct, partner_flipped)):
            remote(
                part_send.at[step, half], part_recv.at[step, half],
                y_send.at[step, half], y_recv.at[step, half], device,
            ).start()
    for step in range(steps):
        columns = pl.ds(step * COLS, COLS)
        part_own[step] = jnp.dot(lhs[1], w_vmem[:, columns], preferred_element_type=F32)

    firsts = (4 - 4 * eta, 4 * eta)
    for step in range(steps):
        columns = pl.ds(step * COLS, COLS)
        for half, device in enumerate((partner_direct, partner_flipped)):
            remote(
                part_send.at[step, half], part_recv.at[step, half],
                y_send.at[step, half], y_recv.at[step, half], device,
            ).wait()
            total = part_own[step, half * ROWS : (half + 1) * ROWS] + part_recv[
                step, half
            ].astype(F32)
            for parity in range(2):
                for near_z in range(2):
                    at = firsts[half] + 2 * near_z + parity
                    row = parity * 16 + near_z * 8
                    out_image[at, :, columns] = total[row : row + 8].astype(BF16)
                    row = 32 + parity * 8 + near_z * 4
                    out_text[at, :, columns] = total[row : row + 4].astype(BF16)

    for n in range(6):
        src, dst = first[n]
        some = dst.at[pl.ds(0, PLANES - 1)]
        remote(some, some, a_send.at[n], a_recv.at[n], z_device(z)).wait_send()
        some = second[n].at[:, pl.ds(0, SLOTS - 1)]
        remote(some, some, b_send.at[n], b_recv.at[n], q_device(q)).wait_send()
    for m, (src, dst) in enumerate(((c_img, d_img), (c_txt, d_txt))):
        some = src.at[pl.ds(0, PLANES - 1)]
        remote(some, some, c_send.at[m], c_recv.at[m], z_device(z)).wait_send()
        some = dst.at[pl.ds(0, SLOTS - 1)]
        remote(some, some, d_send.at[1 - m], d_recv.at[1 - m], q_device(q)).wait_send()


def body(iq, ik, iv, tq, tk, tv, weight, counts, lengths):
    width = weight.shape[1]
    steps = width // COLS

    def planes(tensor):
        return tensor.reshape(PLANES, SLOTS, tensor.shape[2], HD)

    img = pltpu.VMEM((PLANES, SLOTS, IT, HD), BF16)
    txt = pltpu.VMEM((PLANES, SLOTS, TT, HD), BF16)
    dma = pltpu.SemaphoreType.DMA
    anywhere = pl.BlockSpec(memory_space=pl.ANY)
    scalars = pl.BlockSpec(memory_space=pltpu.SMEM)
    vmem = pl.BlockSpec(memory_space=pltpu.VMEM)
    return pl.pallas_call(
        kernel,
        out_shape=(
            jax.ShapeDtypeStruct((8, IT, width), BF16),
            jax.ShapeDtypeStruct((8, TT, width), BF16),
        ),
        in_specs=[anywhere] * 7 + [scalars] * 2,
        out_specs=(vmem, vmem),
        scratch_shapes=[
            *([img, txt] * 3),
            *([img, txt] * 3),
            pltpu.VMEM((KEYS, HD), BF16),
            pltpu.VMEM((KEYS, HD), BF16),
            pltpu.VMEM((PLANES, CHUNK, KEYS), BF16),
            pltpu.VMEM((PLANES, CHUNK, HD), F32),
            img, txt, img, txt,
            pltpu.VMEM((SLOTS, PLANES, IT, HD), BF16),
            pltpu.VMEM((SLOTS, PLANES, TT, HD), BF16),
            pltpu.VMEM(weight.shape, BF16),
            pltpu.VMEM((2, 2 * ROWS, 8 * HD), BF16),
            pltpu.VMEM((steps, 2, ROWS, COLS), BF16),
            pltpu.VMEM((steps, 2, ROWS, COLS), BF16),
            pltpu.VMEM((steps, 2 * ROWS, COLS), F32),
            dma((6,)), dma((6,)), dma((6,)), dma((6,)),
            dma((2,)), dma((2,)), dma((2,)), dma((2,)),
            dma((steps, 2)), dma((steps, 2)), dma, dma((16,)),
        ],
        compiler_params=pltpu.CompilerParams(
            collective_id=0, has_side_effects=True, vmem_limit_bytes=48 * 2**20
        ),
        cost_estimate=pl.CostEstimate(
            flops=2_500_000_000, bytes_accessed=10_000_000, transcendentals=2_400_000
        ),
        name="joint_attention",
    )(planes(iq), planes(ik), planes(iv), planes(tq), planes(tk), planes(tv), weight, counts, lengths)


def solution(mesh):
    tokens = P(None, "head", "seq", None)
    return jax.shard_map(
        body,
        mesh=mesh,
        in_specs=(tokens,) * 6 + (P("head", None), P(), P()),
        out_specs=(P("head", "seq", None), P("head", "seq", None)),
        check_vma=False,
    )
```

time: 229 us -> 88.7 us (0.39)
  Pallas kernels: 0 us -> 79.5 us
  blocking collectives: 70.1 us -> 0 us
  waiting for transfers between devices: 67.7 us -> 0 us
  starting transfers between devices: 42.4 us -> 0 us
  matrix products: 22.5 us -> 0 us
  between operations: 14.2 us -> 0.66 us
  other arithmetic: 7.57 us -> 0 us
  local copies, waits for them, and re-layouts: 2.73 us -> 8.29 us
    pallas_call x0 -> x1, Pallas kernels: none -> 79.5 us  [body(): pl.pallas_call(kernel, out_shape=(jax.ShapeDtypeStruct((8, IT, width), BF...]
    all_to_all x3 -> x0, blocking collectives: 70.1 us -> none  [the longest x1 29.1 us: body(): lax.all_to_all(flatten(text_key), 'seq', split_axis=0, concat_axis=0, til...]
    all_to_all x7 -> x0, waiting for transfers between devices: 67 us -> none  [the longest x1 14.5 us: body(): lax.all_to_all(flatten(image_query), 'seq', split_axis=0, concat_axis=0,...]
    all_to_all x7 -> x0, starting transfers between devices: 42.4 us -> none  [the longest x1 8.18 us: body(): lax.all_to_all(flatten(text_value), 'seq', split_axis=0, concat_axis=0, t...]
    dot_general x14 -> x0, matrix products: 22.5 us -> none  [the longest x1 7.32 us: body(): jnp.einsum('ihtd,hdo->ito', image_part, weight_block, preferred_element_t...]
    unnamed x11 -> x18, local copies, waits for them, and re-layouts: 1.98 us -> 8.29 us
    lt x6 -> x0, other arithmetic: 3.86 us -> none  [the longest x3 2.02 us: body(): image_valid = jnp.arange(key_image.shape[0]) < count_here]
    reduce_sum x8 -> x0, other arithmetic: 3.67 us -> none  [the longest x3 1.72 us: joint_attend(): jnp.sum(image_powers, axis=1, keepdims=True)]
  transfers between devices with their start and end apart: 8 -> 0, of which waited for: 6 -> 0; matrix products, arithmetic and copies ran while one was open for 9% -> 0% of each run, Pallas kernels for 0% -> 0%
where the time goes in v1:
time: 88.7 us; the launch traced here: 88.4 us
  Pallas kernels  79.5 us (90%)
  local copies, waits for them, and re-layouts  8.29 us (9%)
    pallas_call x1, Pallas kernels, body(): pl.pallas_call(kernel, out_shape=(jax.ShapeDtypeStruct((8, IT, width), BF...  79.5 us
    unnamed x18, local copies, waits for them, and re-layouts  8.29 us

profile of v1, /device:TPU:1, one launch (start us, length us, event | category | flops | bytes accessed | tf_op | source)
XLA Modules:
  0.0 88.4 jit_solution(7499636444451430011)
XLA Ops:
  0.6 0.0 copy-start
  0.6 0.9 %copy-done = bf16[16,8,8,128]{3,2,1,0:T(8,128)(2,1)S(1)} copy-done((bf16[16,8,8,128]{3,2,1,0:T(8,128)(2,1)S(1)}, bf16[16,8,8,128]{3,2,1,0:T(8,128)(2,1)}, u32[]{:S(2)}) %copy-start) | copy-done | bytes 262168
  1.6 0.0 copy-start.1
  1.6 0.9 %copy-done.1 = bf16[16,8,8,128]{3,2,1,0:T(8,128)(2,1)S(1)} copy-done((bf16[16,8,8,128]{3,2,1,0:T(8,128)(2,1)S(1)}, bf16[16,8,8,128]{3,2,1,0:T(8,128)(2,1)}, u32[]{:S(2)}) %copy-start.1) | copy-done | bytes 262168
  2.5 0.0 copy-start.2
  2.5 0.9 %copy-done.2 = bf16[16,8,8,128]{3,2,1,0:T(8,128)(2,1)S(1)} copy-done((bf16[16,8,8,128]{3,2,1,0:T(8,128)(2,1)S(1)}, bf16[16,8,8,128]{3,2,1,0:T(8,128)(2,1)}, u32[]{:S(2)}) %copy-start.2) | copy-done | bytes 262168
  3.5 0.0 copy-start.3
  3.5 0.9 %copy-done.3 = bf16[16,8,4,128]{3,2,1,0:T(4,128)(2,1)S(1)} copy-done((bf16[16,8,4,128]{3,2,1,0:T(4,128)(2,1)S(1)}, bf16[16,8,4,128]{3,2,1,0:T(4,128)(2,1)}, u32[]{:S(2)}) %copy-start.3) | copy-done | bytes 131096
  4.4 0.0 copy-start.4
  4.4 0.9 %copy-done.4 = bf16[16,8,4,128]{3,2,1,0:T(4,128)(2,1)S(1)} copy-done((bf16[16,8,4,128]{3,2,1,0:T(4,128)(2,1)S(1)}, bf16[16,8,4,128]{3,2,1,0:T(4,128)(2,1)}, u32[]{:S(2)}) %copy-start.4) | copy-done | bytes 131096
  5.3 0.0 copy-start.5
  5.3 0.9 %copy-done.5 = bf16[16,8,4,128]{3,2,1,0:T(4,128)(2,1)S(1)} copy-done((bf16[16,8,4,128]{3,2,1,0:T(4,128)(2,1)S(1)}, bf16[16,8,4,128]{3,2,1,0:T(4,128)(2,1)}, u32[]{:S(2)}) %copy-start.5) | copy-done | bytes 131096
  6.2 0.0 copy-start.6
  6.2 0.7 copy-done.6
  6.9 0.0 copy-start.7
  6.9 0.7 copy-done.7
  7.5 79.5 %joint_attention.1 = (bf16[8,8,3072]{2,1,0:T(8,128)(2,1)S(1)}, bf16[8,4,3072]{2,1,0:T(4,128)(2,1)S(1)}) custom-call(bf16[8,16,8,128]{3,2,1,0:T(8,128)(2,1)S(1)} %bitcast.6, bf16[8,16,8,128]{3,2,1,0:T(8,128)(2,1)S(1)} %bitcast.7, bf16[8,16,8,128]{3,2,1,0:T(8,128)(2,1)S(1)} %bitcast.8, bf16[8,16,4,128]{3,2,1,0:T(4,128)(2,1)S(1)} %bitcast.9, ...), custom_call_target="tpu_custom_call" | custom-call | flops 2500000000 | bytes 10000000 | tf_op jit(solution)/shard_map/joint_attention/pallas_call | solution.py:314
  87.0 0.7 copy.13
  87.7 0.7 copy.14
Async XLA Ops:
  0.6 1.0 %copy-start = (bf16[16,8,8,128]{3,2,1,0:T(8,128)(2,1)S(1)}, bf16[16,8,8,128]{3,2,1,0:T(8,128)(2,1)}, u32[]{:S(2)}) copy-start(bf16[16,8,8,128]{3,2,1,0:T(8,128)(2,1)} %param.9) | copy-start | bytes 786436
  1.6 0.9 %copy-start.1 = (bf16[16,8,8,128]{3,2,1,0:T(8,128)(2,1)S(1)}, bf16[16,8,8,128]{3,2,1,0:T(8,128)(2,1)}, u32[]{:S(2)}) copy-start(bf16[16,8,8,128]{3,2,1,0:T(8,128)(2,1)} %param.10) | copy-start | bytes 786436
  2.5 0.9 %copy-start.2 = (bf16[16,8,8,128]{3,2,1,0:T(8,128)(2,1)S(1)}, bf16[16,8,8,128]{3,2,1,0:T(8,128)(2,1)}, u32[]{:S(2)}) copy-start(bf16[16,8,8,128]{3,2,1,0:T(8,128)(2,1)} %param.11) | copy-start | bytes 786436
  3.5 0.9 %copy-start.3 = (bf16[16,8,4,128]{3,2,1,0:T(4,128)(2,1)S(1)}, bf16[16,8,4,128]{3,2,1,0:T(4,128)(2,1)}, u32[]{:S(2)}) copy-start(bf16[16,8,4,128]{3,2,1,0:T(4,128)(2,1)} %param.12) | copy-start | bytes 393220
  4.4 0.9 %copy-start.4 = (bf16[16,8,4,128]{3,2,1,0:T(4,128)(2,1)S(1)}, bf16[16,8,4,128]{3,2,1,0:T(4,128)(2,1)}, u32[]{:S(2)}) copy-start(bf16[16,8,4,128]{3,2,1,0:T(4,128)(2,1)} %param.13) | copy-start | bytes 393220
  5.3 0.9 %copy-start.5 = (bf16[16,8,4,128]{3,2,1,0:T(4,128)(2,1)S(1)}, bf16[16,8,4,128]{3,2,1,0:T(4,128)(2,1)}, u32[]{:S(2)}) copy-start(bf16[16,8,4,128]{3,2,1,0:T(4,128)(2,1)} %param.14) | copy-start | bytes 393220
  6.2 0.7 copy-start.6
  6.9 0.7 copy-start.7

commit v2 on v1

v2 whole, which is shorter than its diff:
```python
import jax
import jax.numpy as jnp
from jax import lax
from jax.experimental import pallas as pl
from jax.experimental.pallas import tpu as pltpu
from jax.sharding import PartitionSpec as P

MESH = pl.DeviceIdType.MESH
BF16 = jnp.bfloat16
F32 = jnp.float32

PLANES = 8
SLOTS = 16
HD = 128
IT, TT = 8, 4
IMG_KEYS = PLANES * SLOTS * IT
TXT_KEYS = PLANES * SLOTS * TT
KEYS = IMG_KEYS + TXT_KEYS
COLS = 1024


def merge(block):
    wide = block.astype(F32)
    rows = 1
    for extent in block.shape[:-1]:
        rows *= extent
    return wide.reshape(rows, block.shape[-1]).astype(BF16)


def kernel(
    iq, ik, iv, tq, tk, tv, weight, counts_hbm, lengths_hbm,
    out_image, out_text,
    a_ik, a_tk, a_iv, a_tv, a_iq, a_tq,
    b_ik, b_tk, b_iv, b_tv, b_iq, b_tq,
    keys, values,
    s_img, s_txt, c_img, c_txt, other_img, other_txt, own_img, own_txt,
    w_vmem, lhs_img, lhs_txt, lhs_own,
    send_img, send_txt, recv_img, recv_txt, part_own,
    counts, lengths,
    v_ik, v_tk, v_iv, v_tv, v_iq, v_tq, load_sem,
    a_send, a_recv, b_send, b_recv, c_send, c_recv, d_send, d_recv,
    y_send, y_recv, w_sem, own_sem,
):
    seq = lax.axis_index("seq")
    eta = lax.axis_index("head")
    z = seq // SLOTS
    x, y, c = (seq // 4) % 4, (seq // 2) % 2, seq % 2
    pos = x * 2 + c
    slot = y * 8 + pos
    steps = weight.shape[1] // COLS

    def plane_peer(step):
        return (x + step // 4) % 4, (y + (step // 2) % 2) % 2, (c + step % 2) % 2

    def ring(step):
        return (z + 4 + (step // 2) * (2 * (step % 2) - 1)) % PLANES

    def device(plane, place):
        px, py, pc = place
        return (plane * SLOTS + px * 4 + py * 2 + pc, eta)

    here = (x, y, c)
    planes = [ring(step) for step in range(1, PLANES)]
    places = [plane_peer(step) for step in range(1, SLOTS)]
    row_places = [((x + step // 2) % 4, y, (c + step % 2) % 2) for step in range(1, 8)]

    def z_device(plane):
        return device(plane, here)

    def q_device(place):
        return device(z, place)

    def slot_of(place):
        px, py, pc = place
        return py * 8 + px * 2 + pc

    partners = ((seq, 1 - eta), (seq + 2 - 4 * y, 1 - eta))

    sources = ((ik, v_ik), (tk, v_tk), (iv, v_iv), (tv, v_tv), (iq, v_iq), (tq, v_tq))
    loads = [
        pltpu.make_async_copy(src, dst, load_sem.at[n])
        for n, (src, dst) in enumerate(sources)
    ]
    for copy in loads:
        copy.start()

    barrier = pltpu.get_barrier_semaphore()
    peers = [z_device(plane) for plane in planes]
    peers += [q_device(place) for place in places]
    peers += partners
    for peer in peers:
        pl.semaphore_signal(barrier, inc=1, device_id=peer, device_id_type=MESH)
    pl.semaphore_wait(barrier, len(peers))

    arrivals, departures = {}, []

    def remote(src, dst, send, recv, device):
        return pltpu.make_async_remote_copy(
            src_ref=src, dst_ref=dst, send_sem=send, recv_sem=recv,
            device_id=device, device_id_type=MESH,
        )

    def local(name, src, dst, sem):
        copy = pltpu.make_async_copy(src, dst, sem)
        copy.start()
        arrivals.setdefault(name, []).append(copy.wait)

    def expect(name, some, send, recv):
        copy = remote(some, some, send, recv, partners[0])
        arrivals.setdefault(name, []).append(copy.wait_recv)
        departures.append(copy.wait_send)

    def arrive(name):
        for wait in arrivals.pop(name):
            wait()


    first = ((v_ik, a_ik), (v_tk, a_tk), (v_iv, a_iv), (v_tv, a_tv), (v_iq, a_iq), (v_tq, a_tq))
    second = (b_ik, b_tk, b_iv, b_tv, b_iq, b_tq)

    def start_a(n):
        loads[n].wait()
        src, dst = first[n]
        for plane in planes:
            remote(
                src.at[plane], dst.at[z], a_send.at[n], a_recv.at[n], z_device(plane)
            ).start()
        expect(("a", n), dst.at[pl.ds(0, PLANES - 1)], a_send.at[n], a_recv.at[n])
        local(("a", n), src.at[z], dst.at[z], own_sem.at[n])

    def start_b(n):
        src, dst = first[n][1], second[n]
        for place in places:
            remote(
                src.at[:, slot_of(place)], dst.at[:, slot],
                b_send.at[n], b_recv.at[n], q_device(place),
            ).start()
        expect(("b", n), dst.at[:, pl.ds(0, SLOTS - 1)], b_send.at[n], b_recv.at[n])
        local(("b", n), src.at[:, slot], dst.at[:, slot], own_sem.at[6 + n])

    for n in range(2):
        start_a(n)
    local("weight", weight, w_vmem, w_sem)
    local("scalars", counts_hbm, counts, own_sem.at[16])
    local("scalars", lengths_hbm, lengths, own_sem.at[17])

    for n in range(4):
        arrive(("a", n))
        if n < 3:
            start_a(n + 2)
        start_b(n)

    arrive("scalars")
    image = 2 * z + y
    count, length = counts[image], lengths[image]

    def valid(extent, rows, limit):
        index = lax.broadcasted_iota(jnp.int32, (1, extent), 1)
        at = (index // rows) % SLOTS
        owner = index // (rows * SLOTS) * SLOTS + (at // 2) % 4 * 4 + at // 8 * 2 + at % 2
        return owner * rows + index % rows < limit

    bias = jnp.concatenate(
        [
            jnp.where(valid(IMG_KEYS, IT, count), 0.0, -1e30),
            jnp.where(valid(TXT_KEYS, TT, length), 0.0, -1e30),
        ],
        axis=1,
    ).astype(F32)

    arrive(("b", 0))
    keys[0:IMG_KEYS] = merge(b_ik[...])
    arrive(("b", 1))
    keys[IMG_KEYS:KEYS] = merge(b_tk[...])
    arrive(("b", 2))
    values[0:IMG_KEYS] = merge(b_iv[...])
    arrive(("b", 3))
    values[IMG_KEYS:KEYS] = merge(b_tv[...])

    factor = HD**-0.5 * 1.4426950408889634

    def attend(rows):
        scores = lax.dot_general(
            rows, keys[...], (((1,), (1,)), ((), ())), preferred_element_type=F32
        )
        scores = scores + bias
        highest = jnp.max(scores, axis=1, keepdims=True)
        powers = jnp.exp2((scores - highest) * factor)
        total = jnp.sum(powers, axis=1, keepdims=True)
        mixed = jnp.dot(powers.astype(BF16), values[...], preferred_element_type=F32)
        return mixed * (1.0 / total)

    arrive(("a", 4))
    start_b(4)
    start_a(5)
    arrive(("b", 4))
    arrive(("a", 5))
    start_b(5)

    def image_chunk(step, carry):
        plane = ring(step)
        mixed = attend(merge(b_iq[plane]))
        s_img[plane] = mixed.reshape(2, 8, IT, HD).astype(BF16)
        remote(
            s_img.at[plane], c_img.at[z], c_send.at[0], c_recv.at[0], z_device(plane)
        ).start()
        return carry

    lax.fori_loop(1, PLANES, image_chunk, 0)
    expect(("c", 0), c_img.at[pl.ds(0, PLANES - 1)], c_send.at[0], c_recv.at[0])
    c_img[z] = attend(merge(b_iq[z])).reshape(2, 8, IT, HD).astype(BF16)

    arrive(("b", 5))

    def text_pair(planes):
        rows = [merge(b_tq[plane]) for plane in planes]
        return attend(jnp.concatenate(rows, axis=0)).reshape(2, 2, 8, TT, HD).astype(BF16)

    def send_text(plane, mixed):
        s_txt[plane] = mixed
        remote(
            s_txt.at[plane], c_txt.at[z], c_send.at[1], c_recv.at[1], z_device(plane)
        ).start()

    def text_chunk(step, carry):
        pair = [ring(2 * step + 1 + k) for k in range(2)]
        mixed = text_pair(pair)
        for k in range(2):
            send_text(pair[k], mixed[k])
        return carry

    lax.fori_loop(0, 3, text_chunk, 0)
    mixed = text_pair((planes[6], z))
    send_text(planes[6], mixed[0])
    c_txt[z] = mixed[1]
    expect(("c", 1), c_txt.at[pl.ds(0, PLANES - 1)], c_send.at[1], c_recv.at[1])

    mine, others = pl.ds(4 * eta, 4), pl.ds(4 - 4 * eta, 4)
    spread = ((c_img, other_img, own_img), (c_txt, other_txt, own_txt))
    for n, (src, other, own) in enumerate(spread):
        arrive(("c", n))
        for place in row_places:
            remote(
                src.at[others, :, place[0] * 2 + place[2]], other.at[pos],
                d_send.at[n], d_recv.at[n], q_device(place),
            ).start()
        expect(("d", n), other.at[pl.ds(0, 7)], d_send.at[n], d_recv.at[n])
        local(("d", n), src.at[others, :, pos], other.at[pos], own_sem.at[12 + n])
        for place in places:
            remote(
                src.at[mine, place[1], place[0] * 2 + place[2]], own.at[slot],
                d_send.at[2 + n], d_recv.at[2 + n], q_device(place),
            ).start()
        expect(("d", 2 + n), own.at[pl.ds(0, SLOTS - 1)], d_send.at[2 + n], d_recv.at[2 + n])
        local(("d", 2 + n), src.at[mine, y, pos], own.at[slot], own_sem.at[14 + n])

    arrive("weight")
    sides = (y, 1 - y)
    partial = (
        (other_img, lhs_img, send_img, recv_img), (other_txt, lhs_txt, send_txt, recv_txt)
    )
    for n, (other, lhs, send, recv) in enumerate(partial):
        height = lhs.shape[0] // 2
        arrive(("d", n))
        for half in range(2):
            for head in range(8):
                lhs[
                    half * height : (half + 1) * height, head * HD : (head + 1) * HD
                ] = merge(other[head, :, sides[half]])
        for step in range(steps):
            columns = pl.ds(step * COLS, COLS)
            part = jnp.dot(lhs[...], w_vmem[:, columns], preferred_element_type=F32)
            send[step] = part.astype(BF16).reshape(2, height, COLS)
            for half, partner in enumerate(partners):
                copy = remote(
                    send.at[step, half], recv.at[step, half],
                    y_send.at[n, step, half], y_recv.at[n, step, half], partner,
                )
                copy.start()
                arrivals[("y", n, step, half)] = [copy.wait_recv]
                departures.append(copy.wait_send)

    for n, (own, first_row, height) in enumerate(((own_img, 0, 4 * IT), (own_txt, 8 * IT, 4 * TT))):
        arrive(("d", 2 + n))
        for half in range(2):
            start = first_row + half * height
            for head in range(8):
                lhs_own[start : start + height, head * HD : (head + 1) * HD] = merge(
                    own[sides[half] * 8 + head]
                )
    for step in range(steps):
        columns = pl.ds(step * COLS, COLS)
        part_own[step] = jnp.dot(lhs_own[...], w_vmem[:, columns], preferred_element_type=F32)

    for n, (recv, out, first_row, rows) in enumerate(
        ((recv_img, out_image, 0, IT), (recv_txt, out_text, 8 * IT, TT))
    ):
        for step in range(steps):
            columns = pl.ds(step * COLS, COLS)
            for half in range(2):
                arrive(("y", n, step, half))
                start = first_row + half * 4 * rows
                total = part_own[step, start : start + 4 * rows]
                total = (total + recv[step, half].astype(F32)).reshape(4, rows, COLS)
                for at in range(4):
                    out[2 * at + sides[half], :, columns] = total[at].astype(BF16)
    for wait in departures:
        wait()


def body(iq, ik, iv, tq, tk, tv, weight, counts, lengths):
    width = weight.shape[1]
    steps = width // COLS

    def planes(tensor):
        tensor = tensor.reshape(PLANES, SLOTS, tensor.shape[2], HD)
        return pltpu.with_memory_space_constraint(tensor, pltpu.HBM)

    img = pltpu.VMEM((PLANES, SLOTS, IT, HD), BF16)
    txt = pltpu.VMEM((PLANES, SLOTS, TT, HD), BF16)
    way_img = pltpu.VMEM((PLANES, 2, 8, IT, HD), BF16)
    way_txt = pltpu.VMEM((PLANES, 2, 8, TT, HD), BF16)
    dma = pltpu.SemaphoreType.DMA
    hbm = pl.BlockSpec(memory_space=pltpu.HBM)
    vmem = pl.BlockSpec(memory_space=pltpu.VMEM)
    return pl.pallas_call(
        kernel,
        out_shape=(
            jax.ShapeDtypeStruct((8, IT, width), BF16),
            jax.ShapeDtypeStruct((8, TT, width), BF16),
        ),
        in_specs=[hbm] * 9,
        out_specs=(vmem, vmem),
        scratch_shapes=[
            *([img, txt] * 3),
            *([img, txt] * 3),
            pltpu.VMEM((KEYS, HD), BF16),
            pltpu.VMEM((KEYS, HD), BF16),
            *([way_img, way_txt] * 2),
            pltpu.VMEM((8, 4, 2, IT, HD), BF16), pltpu.VMEM((8, 4, 2, TT, HD), BF16),
            pltpu.VMEM((SLOTS, 4, IT, HD), BF16), pltpu.VMEM((SLOTS, 4, TT, HD), BF16),
            pltpu.VMEM(weight.shape, BF16),
            pltpu.VMEM((8 * IT, 8 * HD), BF16),
            pltpu.VMEM((8 * TT, 8 * HD), BF16),
            pltpu.VMEM((8 * IT + 8 * TT, 8 * HD), BF16),
            *(
                [
                    pltpu.VMEM((steps, 2, 4 * IT, COLS), BF16),
                    pltpu.VMEM((steps, 2, 4 * TT, COLS), BF16),
                ]
                * 2
            ),
            pltpu.VMEM((steps, 8 * IT + 8 * TT, COLS), F32),
            pltpu.SMEM((16,), jnp.int32), pltpu.SMEM((16,), jnp.int32),
            *([img, txt] * 3), dma((6,)),
            dma((6,)), dma((6,)), dma((6,)), dma((6,)),
            dma((2,)), dma((2,)), dma((4,)), dma((4,)),
            dma((2, steps, 2)), dma((2, steps, 2)), dma, dma((18,)),
        ],
        compiler_params=pltpu.CompilerParams(
            collective_id=0, has_side_effects=True, vmem_limit_bytes=40 * 2**20
        ),
        cost_estimate=pl.CostEstimate(
            flops=2_500_000_000, bytes_accessed=10_000_000, transcendentals=2_400_000
        ),
        name="joint_attention",
    )(
        planes(iq), planes(ik), planes(iv), planes(tq), planes(tk), planes(tv),
        pltpu.with_memory_space_constraint(weight, pltpu.HBM),
        pltpu.with_memory_space_constraint(counts, pltpu.HBM),
        pltpu.with_memory_space_constraint(lengths, pltpu.HBM),
    )


def solution(mesh):
    tokens = P(None, "head", "seq", None)
    return jax.shard_map(
        body,
        mesh=mesh,
        in_specs=(tokens,) * 6 + (P("head", None), P(), P()),
        out_specs=(P("head", "seq", None), P("head", "seq", None)),
        check_vma=False,
    )
```

time: 88.7 us -> 69.2 us (0.78)
  Pallas kernels: 79.5 us -> 67 us
  local copies, waits for them, and re-layouts: 8.29 us -> 1.42 us
    pallas_call x1, Pallas kernels: 79.5 us -> 67 us  [body(): pl.pallas_call(kernel, out_shape=(jax.ShapeDtypeStruct((8, IT, width), BF...]
    unnamed x18 -> x2, local copies, waits for them, and re-layouts: 8.29 us -> 1.42 us
where the time goes in v2:
time: 69.2 us; the launch traced here: 69.1 us
  Pallas kernels  67 us (97%)
  local copies, waits for them, and re-layouts  1.42 us (2%)
    pallas_call x1, Pallas kernels, body(): pl.pallas_call(kernel, out_shape=(jax.ShapeDtypeStruct((8, IT, width), BF...  67 us
    unnamed x2, local copies, waits for them, and re-layouts  1.42 us

profile of v2, /device:TPU:1, one launch (start us, length us, event | category | flops | bytes accessed | tf_op | source)
XLA Modules:
  0.0 69.1 jit_solution(14522135300370696880)
XLA Ops:
  0.6 67.0 %joint_attention.1 = (bf16[8,8,3072]{2,1,0:T(8,128)(2,1)S(1)}, bf16[8,4,3072]{2,1,0:T(4,128)(2,1)S(1)}) custom-call(bf16[8,16,8,128]{3,2,1,0:T(8,128)(2,1)} %bitcast.6, bf16[8,16,8,128]{3,2,1,0:T(8,128)(2,1)} %bitcast.7, bf16[8,16,8,128]{3,2,1,0:T(8,128)(2,1)} %bitcast.8, bf16[8,16,4,128]{3,2,1,0:T(4,128)(2,1)} %bitcast.9, bf16[8,16,4,128]{3,2,1,0:T(4,128)(2,1)} %bitcast.10, ...), custom_call_target="tpu_custom_call" | custom-call | flops 2500000000 | bytes 10000000 | tf_op jit(solution)/shard_map/joint_attention/pallas_call | solution.py:326
  67.6 0.7 %copy.13 = bf16[8,8,3072]{2,1,0:T(8,128)(2,1)} copy(bf16[8,8,3072]{2,1,0:T(8,128)(2,1)S(1)} %get-tuple-element.4) | data formatting | bytes 786432
  68.4 0.7 copy.14

commit v3 on v2

--- a/solution.py
+++ b/solution.py
@@ -76,7 +76,7 @@
 
     partners = ((seq, 1 - eta), (seq + 2 - 4 * y, 1 - eta))
 
-    sources = ((ik, v_ik), (tk, v_tk), (iv, v_iv), (tv, v_tv), (iq, v_iq), (tq, v_tq))
+    sources = ((ik, v_ik), (tk, v_tk), (iv, v_iv), (tv, v_tv), (tq, v_tq), (iq, v_iq))
     loads = [
         pltpu.make_async_copy(src, dst, load_sem.at[n])
         for n, (src, dst) in enumerate(sources)
@@ -115,8 +115,8 @@
             wait()
 
 
-    first = ((v_ik, a_ik), (v_tk, a_tk), (v_iv, a_iv), (v_tv, a_tv), (v_iq, a_iq), (v_tq, a_tq))
-    second = (b_ik, b_tk, b_iv, b_tv, b_iq, b_tq)
+    first = ((v_ik, a_ik), (v_tk, a_tk), (v_iv, a_iv), (v_tv, a_tv), (v_tq, a_tq), (v_iq, a_iq))
+    second = (b_ik, b_tk, b_iv, b_tv, b_tq, b_iq)
 
     def start_a(n):
         loads[n].wait()
@@ -146,8 +146,7 @@
 
     for n in range(4):
         arrive(("a", n))
-        if n < 3:
-            start_a(n + 2)
+        start_a(n + 2)
         start_b(n)
 
     arrive("scalars")
@@ -192,10 +191,34 @@
 
     arrive(("a", 4))
     start_b(4)
-    start_a(5)
     arrive(("b", 4))
     arrive(("a", 5))
     start_b(5)
+
+    def text_pair(planes):
+        rows = [merge(b_tq[plane]) for plane in planes]
+        return attend(jnp.concatenate(rows, axis=0)).reshape(2, 2, 8, TT, HD).astype(BF16)
+
+    def send_text(plane, mixed):
+        s_txt[plane] = mixed
+        remote(
+            s_txt.at[plane], c_txt.at[z], c_send.at[1], c_recv.at[1], z_device(plane)
+        ).start()
+
+    def text_chunk(step, carry):
+        pair = [ring(2 * step + 1 + k) for k in range(2)]
+        mixed = text_pair(pair)
+        for k in range(2):
+            send_text(pair[k], mixed[k])
+        return carry
+
+    lax.fori_loop(0, 3, text_chunk, 0)
+    mixed = text_pair((planes[6], z))
+    send_text(planes[6], mixed[0])
+    c_txt[z] = mixed[1]
+    expect(("c", 1), c_txt.at[pl.ds(0, PLANES - 1)], c_send.at[1], c_recv.at[1])
+
+    arrive(("b", 5))
 
     def image_chunk(step, carry):
         plane = ring(step)
@@ -210,34 +233,10 @@
     expect(("c", 0), c_img.at[pl.ds(0, PLANES - 1)], c_send.at[0], c_recv.at[0])
     c_img[z] = attend(merge(b_iq[z])).reshape(2, 8, IT, HD).astype(BF16)
 
-    arrive(("b", 5))
-
-    def text_pair(planes):
-        rows = [merge(b_tq[plane]) for plane in planes]
-        return attend(jnp.concatenate(rows, axis=0)).reshape(2, 2, 8, TT, HD).astype(BF16)
-
-    def send_text(plane, mixed):
-        s_txt[plane] = mixed
-        remote(
-            s_txt.at[plane], c_txt.at[z], c_send.at[1], c_recv.at[1], z_device(plane)
-        ).start()
-
-    def text_chunk(step, carry):
-        pair = [ring(2 * step + 1 + k) for k in range(2)]
-        mixed = text_pair(pair)
-        for k in range(2):
-            send_text(pair[k], mixed[k])
-        return carry
-
-    lax.fori_loop(0, 3, text_chunk, 0)
-    mixed = text_pair((planes[6], z))
-    send_text(planes[6], mixed[0])
-    c_txt[z] = mixed[1]
-    expect(("c", 1), c_txt.at[pl.ds(0, PLANES - 1)], c_send.at[1], c_recv.at[1])
-
     mine, others = pl.ds(4 * eta, 4), pl.ds(4 - 4 * eta, 4)
     spread = ((c_img, other_img, own_img), (c_txt, other_txt, own_txt))
-    for n, (src, other, own) in enumerate(spread):
+    for n in (1, 0):
+        src, other, own = spread[n]
         arrive(("c", n))
         for place in row_places:
             remote(
@@ -259,7 +258,8 @@
     partial = (
         (other_img, lhs_img, send_img, recv_img), (other_txt, lhs_txt, send_txt, recv_txt)
     )
-    for n, (other, lhs, send, recv) in enumerate(partial):
+    for n in (1, 0):
+        other, lhs, send, recv = partial[n]
         height = lhs.shape[0] // 2
         arrive(("d", n))
         for half in range(2):
@@ -292,9 +292,9 @@
         columns = pl.ds(step * COLS, COLS)
         part_own[step] = jnp.dot(lhs_own[...], w_vmem[:, columns], preferred_element_type=F32)
 
-    for n, (recv, out, first_row, rows) in enumerate(
-        ((recv_img, out_image, 0, IT), (recv_txt, out_text, 8 * IT, TT))
-    ):
+    last = ((recv_img, out_image, 0, IT), (recv_txt, out_text, 8 * IT, TT))
+    for n in (1, 0):
+        recv, out, first_row, rows = last[n]
         for step in range(steps):
             columns = pl.ds(step * COLS, COLS)
             for half in range(2):

time: 69.2 us -> 72.3 us (1.045)
  Pallas kernels: 67 us -> 70.2 us
    pallas_call x1, Pallas kernels: 67 us -> 70.2 us  [body(): pl.pallas_call(kernel, out_shape=(jax.ShapeDtypeStruct((8, IT, width), BF...]
where the time goes in v3:
time: 72.3 us
  Pallas kernels  70.2 us (97%)
  local copies, waits for them, and re-layouts  1.42 us (2%)
    pallas_call x1, Pallas kernels, body(): pl.pallas_call(kernel, out_shape=(jax.ShapeDtypeStruct((8, IT, width), BF...  70.2 us

profile of v3, /device:TPU:1, one launch (start us, length us, event | category | flops | bytes accessed | tf_op | source)
XLA Modules:
  0.0 72.3 jit_solution(7105764453277227204)
XLA Ops:
  0.6 70.2 %joint_attention.1 = (bf16[8,8,3072]{2,1,0:T(8,128)(2,1)S(1)}, bf16[8,4,3072]{2,1,0:T(4,128)(2,1)S(1)}) custom-call(bf16[8,16,8,128]{3,2,1,0:T(8,128)(2,1)} %bitcast.6, bf16[8,16,8,128]{3,2,1,0:T(8,128)(2,1)} %bitcast.7, bf16[8,16,8,128]{3,2,1,0:T(8,128)(2,1)} %bitcast.8, bf16[8,16,4,128]{3,2,1,0:T(4,128)(2,1)} %bitcast.9, bf16[8,16,4,128]{3,2,1,0:T(4,128)(2,1)} %bitcast.10, ...), custom_call_target="tpu_custom_call" | custom-call | flops 2500000000 | bytes 10000000 | tf_op jit(solution)/shard_map/joint_attention/pallas_call | solution.py:326
  70.8 0.7 %copy.13 = bf16[8,8,3072]{2,1,0:T(8,128)(2,1)} copy(bf16[8,8,3072]{2,1,0:T(8,128)(2,1)S(1)} %get-tuple-element.4) | data formatting | bytes 786432
  71.6 0.7 copy.14

commit v4 on v3

--- a/solution.py
+++ b/solution.py
@@ -191,9 +191,9 @@
 
     arrive(("a", 4))
     start_b(4)
-    arrive(("b", 4))
     arrive(("a", 5))
     start_b(5)
+    arrive(("b", 4))
 
     def text_pair(planes):
         rows = [merge(b_tq[plane]) for plane in planes]

time: 72.3 us -> 68.7 us (0.950)
  Pallas kernels: 70.2 us -> 66.5 us
    pallas_call x1, Pallas kernels: 70.2 us -> 66.5 us  [body(): pl.pallas_call(kernel, out_shape=(jax.ShapeDtypeStruct((8, IT, width), BF...]
where the time goes in v4:
time: 68.7 us; the launch traced here: 68.6 us
  Pallas kernels  66.5 us (97%)
  local copies, waits for them, and re-layouts  1.42 us (2%)
    pallas_call x1, Pallas kernels, body(): pl.pallas_call(kernel, out_shape=(jax.ShapeDtypeStruct((8, IT, width), BF...  66.5 us
    unnamed x2, local copies, waits for them, and re-layouts  1.42 us

profile of v4, /device:TPU:1, one launch (start us, length us, event | category | flops | bytes accessed | tf_op | source)
XLA Modules:
  0.0 68.6 jit_solution(10490284428265501164)
XLA Ops:
  0.6 66.5 %joint_attention.1 = (bf16[8,8,3072]{2,1,0:T(8,128)(2,1)S(1)}, bf16[8,4,3072]{2,1,0:T(4,128)(2,1)S(1)}) custom-call(bf16[8,16,8,128]{3,2,1,0:T(8,128)(2,1)} %bitcast.6, bf16[8,16,8,128]{3,2,1,0:T(8,128)(2,1)} %bitcast.7, bf16[8,16,8,128]{3,2,1,0:T(8,128)(2,1)} %bitcast.8, bf16[8,16,4,128]{3,2,1,0:T(4,128)(2,1)} %bitcast.9, bf16[8,16,4,128]{3,2,1,0:T(4,128)(2,1)} %bitcast.10, ...), custom_call_target="tpu_custom_call" | custom-call | flops 2500000000 | bytes 10000000 | tf_op jit(solution)/shard_map/joint_attention/pallas_call | solution.py:326
  67.2 0.7 %copy.13 = bf16[8,8,3072]{2,1,0:T(8,128)(2,1)} copy(bf16[8,8,3072]{2,1,0:T(8,128)(2,1)S(1)} %get-tuple-element.4) | data formatting | bytes 786432
  67.9 0.7 copy.14
